TPU v7x, 256 devices: a whole 4x4x8 slice. The times are simulated.
256 devices in a mesh: fsdp: 64 (over x, z, core), group: 4 (over y).
Axes of the slice: x: 4, y: 4, z: 8, core: 2. Of those that a mesh axis runs over, the one named last changes fastest.
Arguments:
- weights: bfloat16 [16, 3072, 4096], P('group', 'fsdp')
- placement: int32 [4, 20], P('group'), may hold values from 0 to 15, as said below
Outputs:
- rollout_codes: bfloat16 [4, 16384, 5, 3072], P('group', 'fsdp')
- rollout_scales: float32 [4, 20, 24, 32], P('group')
Inputs may be any that keep to these rules, and one draw needn't show every extreme that they name: `placement`: in each row of the table the first 16 slots name every expert once; the last 4 slots name replicas drawn from 4 experts of that row.
All inputs are finite; a program needn't handle non-finite values.
Results may differ from a plain program's by a relative error of at most 0.001.
Values may be sent and summed in bfloat16 or wider, within the bound.
A program may use at most 128 MiB of HBM per device.

v0:
```python
import jax
import jax.numpy as jnp
from jax import lax
from jax.sharding import PartitionSpec as P

TILE = 128
OWNERS = 4


EPSILON = 1e-06


def on_device(weights, placement):
    groups_here, shard_rows, columns = weights.shape
    tile_size = TILE
    devices = lax.axis_size("fsdp")
    position = lax.axis_index("fsdp")
    owner_count = OWNERS
    col_owners = devices // owner_count
    col_width = columns // col_owners
    row_tiles = devices * shard_rows // tile_size
    col_tiles = columns // tile_size
    magnitude = jnp.max(
        jnp.abs(weights).reshape(groups_here, shard_rows, col_tiles, tile_size), axis=3
    ).astype(jnp.float32)
    row_ids = (position * shard_rows + jnp.arange(shard_rows, dtype=jnp.int32)) // tile_size
    member = row_ids[:, None] == jnp.arange(row_tiles, dtype=jnp.int32)[None, :]
    partial_max = jnp.max(
        jnp.where(member[None, :, :, None], magnitude[:, :, None, :], 0.0), axis=1
    )
    tile_max = lax.pmax(partial_max, "fsdp")
    row_max = jnp.sum(jnp.where(member[None, :, :, None], tile_max[:, None, :, :], 0.0), axis=2)
    scaled = weights.astype(jnp.float32).reshape(groups_here, shard_rows, col_tiles, tile_size) / (
        row_max[..., None] + EPSILON
    )
    code_tiles = scaled.reshape(groups_here, shard_rows, columns).astype(jnp.bfloat16)
    all_scales = lax.all_gather(tile_max, "group", axis=0, tiled=True)
    slot_list = placement[0]
    slot_count = slot_list.shape[0]
    slot_own = slot_count // owner_count
    rollout_scales = jnp.take(all_scales, slot_list, axis=0)[None]
    every_code = lax.all_gather(code_tiles, "group", axis=0, tiled=True)
    chosen = jnp.take(every_code, slot_list, axis=0)
    chosen = chosen.reshape(owner_count, slot_own, shard_rows, col_owners, col_width)
    outgoing = jnp.transpose(chosen, (0, 3, 1, 2, 4)).reshape(
        devices, slot_own, shard_rows, col_width
    )
    arrived = lax.all_to_all(outgoing, "fsdp", split_axis=0, concat_axis=0, tiled=True)
    owned_codes = jnp.transpose(arrived, (3, 1, 0, 2)).reshape(
        col_width, slot_own, devices * shard_rows
    )
    return (owned_codes[None], rollout_scales)


def solution(mesh):
    in_specs = (P("group", "fsdp", None), P("group", None))
    out_specs = (P("group", "fsdp", None, None), P("group", None, None, None))
    return jax.shard_map(
        on_device, mesh=mesh, in_specs=in_specs, out_specs=out_specs, check_vma=False
    )
```

profile of v0, /device:TPU:128, one launch (start us, length us, event | category | flops | bytes accessed | tf_op | source)
XLA Modules:
  0.0 568.0 jit_solution(3717322648172075429)
XLA Ops:
  7.2 0.0 all-gather.2.cloned.1.call-start
  7.2 1.7 abs.3
  9.0 0.3 copy.25
  9.3 0.9 bitcast_reduce_fusion
  10.2 0.1 copy.20
  10.3 0.5 select_reduce_fusion.1
  10.8 231.7 %pmax.7 = f32[4,24,32]{2,1,0:T(8,128)S(1)} all-reduce(f32[4,24,32]{2,1,0:T(8,128)S(1)} %select_reduce_fusion.1), channel_id=1, replica_groups=mesh['fsdp'=64,'group'=4] {'fsdp'}, use_global_device_ids=true, to_apply=%region_2.3 | all-reduce | flops 3072 | bytes 24576 | tf_op jit(solution)/shard_map/pmax | solution.py:31
  242.5 0.5 select_reduce_fusion
  243.0 0.1 copy.21
  243.1 0.9 div.27
  244.0 2.3 div.28
  246.3 0.0 copy-start
  246.3 4.0 divide_convert_fusion
  250.3 0.0 all-gather.2.cloned.1.call-update
  250.4 0.5 broadcast.128
  250.9 0.0 copy-done
  250.9 0.7 reduce.3
  251.5 0.1 squeeze.7
  251.7 81.5 %all-gather.2.cloned.1.call-done = bf16[16,48,4096]{2,1,0:T(8,128)(2,1)} async-done(((bf16[4,48,4096]{2,1,0:T(8,128)(2,1)}), bf16[16,48,4096]{2,1,0:T(8,128)(2,1)}) %all-gather.2.cloned.1.call-update) | async-done | bytes 6291472 | tf_op jit(solution)/shard_map/all_gather | solution.py:42
  333.1 8.1 %gather_fusion = bf16[20,48,4096]{2,1,0:T(8,128)(2,1)} fusion(bf16[16,48,4096]{2,1,0:T(8,128)(2,1)} %all-gather.2.cloned.1.call-done, s32[1024]{0:T(1024)S(1)} %pad_clamp_fusion), kind=kCustom, calls=%fused_computation | custom fusion | bytes 15728720 | tf_op jit(solution)/shard_map/jit(_take)/gather | solution.py:43
  341.3 6.1 %copy.26 = bf16[120,8,16,256]{3,2,1,0:T(8,128)(2,1)S(1)} copy(bf16[120,8,16,256]{3,1,2,0:T(8,128)(2,1)} %bitcast.27) | data formatting | bytes 15728640
  347.4 4.0 select_bitcast_fusion
  351.4 9.5 %copy.22 = bf16[4,16,5,48,256]{4,3,2,1,0:T(8,128)(2,1)} copy(bf16[4,16,5,48,256]{4,1,3,2,0:T(8,128)(2,1)} %select_bitcast_fusion) | data formatting | bytes 15728640 | tf_op jit(solution)/shard_map/transpose | solution.py:45
  360.9 10.3 %all-to-all-start = ((bf16[64,5,48,256]{3,2,1,0:T(8,128)(2,1)}), bf16[64,5,48,256]{3,2,1,0:T(8,128)(2,1)}, u32[]{:S(2)}, u32[]{:S(2)}) async-start(bf16[64,5,48,256]{3,2,1,0:T(8,128)(2,1)} %bitcast.28), calls=%async_computation | async-start | bytes 15728640 | tf_op jit(solution)/shard_map/all_to_all | solution.py:48
  371.3 12.1 %all_gather.7 = f32[16,24,32]{2,1,0:T(8,128)S(1)} all-gather(f32[4,24,32]{2,1,0:T(8,128)S(1)} %pmax.7), channel_id=1, replica_groups=mesh['fsdp'=64,'group'=4] {'group'}, dimensions={0}, use_global_device_ids=true | all-gather | bytes 61440 | tf_op jit(solution)/shard_map/all_gather | solution.py:37
  383.4 0.6 gather_fusion.1
  384.0 0.8 bitcast_select_fusion
  384.8 158.6 %all-to-all-done = bf16[64,5,48,256]{3,2,1,0:T(8,128)(2,1)} async-done(((bf16[64,5,48,256]{3,2,1,0:T(8,128)(2,1)}), bf16[64,5,48,256]{3,2,1,0:T(8,128)(2,1)}, u32[]{:S(2)}, u32[]{:S(2)}) %all-to-all-start) | async-done | bytes 7864352 | tf_op jit(solution)/shard_map/all_to_all | solution.py:48
  543.4 7.1 %copy.23 = bf16[64,5,48,256]{3,2,0,1:T(8,128)(2,1)} copy(bf16[64,5,48,256]{3,2,1,0:T(8,128)(2,1)} %all-to-all-done) | data formatting | bytes 15728640 | tf_op jit(solution)/shard_map/all_to_all | solution.py:48
  550.6 10.6 %copy.24 = bf16[1,256,5,3072]{3,1,2,0:T(8,128)(2,1)} copy(bf16[1,256,5,3072]{1,3,2,0:T(8,128)(2,1)} %bitcast.29) | data formatting | bytes 15728640
  (8 shorter events, 0.1 us)
Async XLA Ops:
  7.2 326.0 %all-gather.2.cloned.1.call-start = ((), (), s32[]{:S(2)}) async-start(), calls=%async_computation.1 | async-start | bytes 7864320 | tf_op jit(solution)/shard_map/all_gather | solution.py:42
  246.3 4.5 copy-start
  360.9 182.5 %all-to-all-start = ((bf16[64,5,48,256]{3,2,1,0:T(8,128)(2,1)}), bf16[64,5,48,256]{3,2,1,0:T(8,128)(2,1)}, u32[]{:S(2)}, u32[]{:S(2)}) async-start(bf16[64,5,48,256]{3,2,1,0:T(8,128)(2,1)} %bitcast.28), calls=%async_computation | async-start | bytes 15728640 | tf_op jit(solution)/shard_map/all_to_all | solution.py:48
Sparse Core Ops, SparseCore 0:
  250.5 82.5 all-gather.1
where the time goes:
time: 574 us; the launch traced here: 568 us
  blocking collectives  244 us (43%)
  waiting for transfers between devices  240 us (42%)
  local copies, waits for them, and re-layouts  46.4 us (8%)
  between operations  14.1 us (2%)
  other arithmetic  13.1 us (2%)
  starting transfers between devices  10.4 us (2%)
    pmax x1, blocking collectives, on_device(): tile_max = lax.pmax(partial_max, 'fsdp')  232 us
    all_to_all x1, waiting for transfers between devices, on_device(): lax.all_to_all(outgoing, 'fsdp', split_axis=0, concat_axis=0, tiled=True)  159 us
    all_gather x1, waiting for transfers between devices, on_device(): every_code = lax.all_gather(code_tiles, 'group', axis=0, tiled=True)  81.5 us
    unnamed x6, local copies, waits for them, and re-layouts  17.6 us
    all_gather x1, blocking collectives, on_device(): all_scales = lax.all_gather(tile_max, 'group', axis=0, tiled=True)  12.1 us
  transfers between devices with their start and end apart: 2, of which 2 were waited for; matrix products, arithmetic and copies ran while one was open for 0% of the time, Pallas kernels for 0%

commit v1 on v0

v1 whole, which is shorter than its diff:
```python
import functools

import jax
import jax.numpy as jnp
from jax import lax
from jax.experimental import pallas as pl
from jax.experimental.pallas import tpu as pltpu
from jax.sharding import PartitionSpec as P

MESH = pl.DeviceIdType.MESH
TILE = 128
EPSILON = 1e-6
NX, NY, NZ = 4, 4, 8
NC = 16
EXPERTS_HERE = 4
SLOTS_OWN = 5
ROWS_HERE = 48
ROW_TILES = 6
CHUNKS = 2 * ROW_TILES
Z_ORDER = [(0, 1)] + [(dz, dc) for dz in (1, 7, 2, 6, 3, 5, 4) for dc in (0, 1)]
X_ORDER = (2, 1, 3)
Y_ORDER = (2, 1, 3)


def comm_kernel(w_ref, place_ref, out_ref, scales_ref, *scratch):
    ybufs = scratch[:CHUNKS]
    (zbuf, staged, acc, zmax, ymax, xmax,
     z_send, z_recv, y_send, y_recv, x_send, x_recv, own_sem,
     sz_send, sz_recv, sy_send, sy_recv, sx_send, sx_recv) = scratch[CHUNKS:]
    f = lax.axis_index("fsdp")
    y = lax.axis_index("group")
    x = f // NC
    c = f % NC
    z = c // 2
    core = c % 2

    def z_dev(step):
        dz, dc = step
        return 2 * ((z + dz) % NZ) + (core + dc) % 2

    def y_dev(dy):
        return (y + dy) % NY

    def x_dev(dx):
        return (x + dx) % NX

    barrier = pltpu.get_barrier_semaphore()
    for step in Z_ORDER:
        pl.semaphore_signal(barrier, inc=1, device_id=(x * NC + z_dev(step), y), device_id_type=MESH)
    for d in Y_ORDER:
        pl.semaphore_signal(barrier, inc=1, device_id=(f, y_dev(d)), device_id_type=MESH)
    for d in X_ORDER:
        pl.semaphore_signal(barrier, inc=1, device_id=(x_dev(d) * NC + c, y), device_id_type=MESH)
    pl.semaphore_wait(barrier, len(Z_ORDER) + len(Y_ORDER) + len(X_ORDER))

    waits = []

    def z_copy(k, ct):
        to = z_dev(Z_ORDER[k])
        cols = pl.ds(pl.multiple_of(to * (2 * TILE) + ct * TILE, TILE), TILE)
        rows = pl.ds(pl.multiple_of(c * ROWS_HERE, 16), ROWS_HERE)
        return pltpu.make_async_remote_copy(
            src_ref=w_ref.at[:, :, cols],
            dst_ref=zbuf.at[ct, :, rows, :],
            send_sem=z_send.at[ct, k],
            recv_sem=z_recv.at[ct, c],
            device_id=(x * NC + to, y),
            device_id_type=MESH,
        )

    def z_start(k, ct):
        copy = z_copy(k, ct)
        copy.start()
        waits.append(copy)

    for ct in range(2):
        cols = pl.ds(pl.multiple_of(c * (2 * TILE) + ct * TILE, TILE), TILE)
        rows = pl.ds(pl.multiple_of(c * ROWS_HERE, 16), ROWS_HERE)
        pltpu.make_async_copy(w_ref.at[:, :, cols], zbuf.at[ct, :, rows, :], z_recv.at[ct, c]).start()
        for k in range(5):
            z_start(k, ct)
    for k in range(5, len(Z_ORDER)):
        for ct in range(2):
            z_start(k, ct)

    def z_wait(ct, first, last):
        def body(s, carry):
            rows = pl.ds(pl.multiple_of(s * ROWS_HERE, 16), ROWS_HERE)
            part = zbuf.at[ct, :, rows, :]
            pltpu.make_async_copy(part, part, z_recv.at[ct, s]).wait()
            return carry

        lax.fori_loop(first, last, body, 0)

    tile0 = (3 * z) // 4

    def tile_of(i):
        return (tile0 + i // 2) % ROW_TILES

    def first_source(t):
        return (8 * t) // 3

    def end_source(t):
        return (8 * t + 7) // 3 + 1

    acc[...] = jnp.zeros_like(acc)
    lane = lax.broadcasted_iota(jnp.int32, acc.shape, 1)
    sub = lax.broadcasted_iota(jnp.int32, acc.shape, 0)

    def y_copy(i, n):
        here = pl.ds(y * EXPERTS_HERE, EXPERTS_HERE)
        return pltpu.make_async_remote_copy(
            src_ref=ybufs[i].at[here],
            dst_ref=ybufs[i].at[here],
            send_sem=y_send.at[i, n],
            recv_sem=y_recv.at[i, n],
            device_id=(f, y_dev(Y_ORDER[n])),
            device_id_type=MESH,
        )

    def scale_and_send(i):
        order, ct = i // 2, i % 2
        t = tile_of(i)
        first, last = first_source(t), end_source(t)
        if order > 0:
            first = jnp.where(t > 0, jnp.maximum(first, end_source(t - 1)), first)
        if order == ROW_TILES - 1:
            last = jnp.where(t + 1 == tile0, jnp.minimum(last, first_source(tile0)), last)
        z_wait(ct, first, last)
        rows = pl.ds(pl.multiple_of(t * TILE, TILE), TILE)
        total = acc[...]
        for e in range(EXPERTS_HERE):
            block = zbuf[ct, e, rows, :].astype(jnp.float32)
            top = jnp.max(jnp.max(jnp.abs(block), axis=0, keepdims=True), axis=1, keepdims=True)
            code = (block / (top + EPSILON)).astype(jnp.bfloat16)
            ybufs[i][y * EXPERTS_HERE + e] = code.T
            at = (sub == t) & (lane == e * 32 + 2 * c + ct)
            total = jnp.where(at, top, total)
        acc[...] = total
        for n in range(3):
            copy = y_copy(i, n)
            copy.start()
            waits.append(copy)

    def select_and_send(i):
        ct = i % 2
        t = tile_of(i)
        for n, d in enumerate(Y_ORDER):
            there = pl.ds(((y - d) % NY) * EXPERTS_HERE, EXPERTS_HERE)
            part = ybufs[i].at[there]
            pltpu.make_async_copy(part, part, y_recv.at[i, n]).wait()
        for n, d in enumerate(X_ORDER + (0,)):
            owner = x_dev(d)
            for j in range(SLOTS_OWN):
                expert = place_ref[0, owner * SLOTS_OWN + j]
                staged[i, n, j] = ybufs[i][expert]
            target = out_ref.at[x * ROW_TILES + t, ct]
            if d:
                copy = pltpu.make_async_remote_copy(
                    src_ref=staged.at[i, n],
                    dst_ref=target,
                    send_sem=x_send.at[i, n],
                    recv_sem=x_recv.at[i, n],
                    device_id=(owner * NC + c, y),
                    device_id_type=MESH,
                )
                copy.start()
                waits.append(copy)
            else:
                pltpu.make_async_copy(staged.at[i, n], target, own_sem.at[i]).start()

    for i in range(CHUNKS + 1):
        if i < CHUNKS:
            scale_and_send(i)
        if i >= 1:
            select_and_send(i - 1)

    zmax[c] = acc[...]
    for k, step in enumerate(Z_ORDER):
        pltpu.make_async_remote_copy(
            src_ref=zmax.at[c], dst_ref=zmax.at[c], send_sem=sz_send.at[k], recv_sem=sz_recv.at[c],
            device_id=(x * NC + z_dev(step), y), device_id_type=MESH,
        ).start()
    for k, step in enumerate(Z_ORDER):
        source = z_dev(step)
        part = zmax.at[source]
        pltpu.make_async_copy(part, part, sz_recv.at[source]).wait()
        pltpu.make_async_copy(part, part, sz_send.at[k]).wait()
    ymax[y] = jnp.max(zmax[...], axis=0)
    for n, d in enumerate(Y_ORDER):
        pltpu.make_async_remote_copy(
            src_ref=ymax.at[y], dst_ref=ymax.at[y], send_sem=sy_send.at[n], recv_sem=sy_recv.at[n],
            device_id=(f, y_dev(d)), device_id_type=MESH,
        ).start()
    for n, d in enumerate(Y_ORDER):
        part = ymax.at[(y - d) % NY]
        pltpu.make_async_copy(part, part, sy_recv.at[n]).wait()
        pltpu.make_async_copy(part, part, sy_send.at[n]).wait()
    xmax[x] = ymax[...]
    for n, d in enumerate(X_ORDER):
        pltpu.make_async_remote_copy(
            src_ref=xmax.at[x], dst_ref=xmax.at[x], send_sem=sx_send.at[n], recv_sem=sx_recv.at[n],
            device_id=(x_dev(d) * NC + c, y), device_id_type=MESH,
        ).start()
    for n, d in enumerate(X_ORDER):
        part = xmax.at[(x - d) % NX]
        pltpu.make_async_copy(part, part, sx_recv.at[n]).wait()
        pltpu.make_async_copy(part, part, sx_send.at[n]).wait()
    scales_ref[...] = xmax[...]

    for copy in waits:
        copy.wait_send()
    for i in range(CHUNKS):
        ct = i % 2
        t = tile_of(i)
        for n, d in enumerate(X_ORDER):
            part = out_ref.at[((x - d) % NX) * ROW_TILES + t, ct]
            pltpu.make_async_copy(part, part, x_recv.at[i, n]).wait()
        mine = out_ref.at[x * ROW_TILES + t, ct]
        pltpu.make_async_copy(staged.at[i, 3], mine, own_sem.at[i]).wait()


def exchange(weights, placement):
    sem = pltpu.SemaphoreType.DMA
    return pl.pallas_call(
        comm_kernel,
        out_shape=(
            jax.ShapeDtypeStruct((NX * ROW_TILES, 2, SLOTS_OWN, TILE, TILE), jnp.bfloat16),
            jax.ShapeDtypeStruct((NX, NY, 8, TILE), jnp.float32),
        ),
        in_specs=[pl.BlockSpec(memory_space=pl.ANY), pl.BlockSpec(memory_space=pltpu.SMEM)],
        out_specs=(pl.BlockSpec(memory_space=pl.ANY), pl.BlockSpec(memory_space=pltpu.VMEM)),
        scratch_shapes=[pltpu.VMEM((16, TILE, TILE), jnp.bfloat16)] * CHUNKS
        + [
            pltpu.VMEM((2, EXPERTS_HERE, ROW_TILES * TILE, TILE), jnp.bfloat16),
            pltpu.VMEM((CHUNKS, 4, SLOTS_OWN, TILE, TILE), jnp.bfloat16),
            pltpu.VMEM((8, TILE), jnp.float32),
            pltpu.VMEM((NC, 8, TILE), jnp.float32),
            pltpu.VMEM((NY, 8, TILE), jnp.float32),
            pltpu.VMEM((NX, NY, 8, TILE), jnp.float32),
            sem((2, 15)), sem((2, NC)),
            sem((CHUNKS, 3)), sem((CHUNKS, 3)),
            sem((CHUNKS, 3)), sem((CHUNKS, 3)), sem((CHUNKS,)),
            sem((15,)), sem((NC,)),
            sem((3,)), sem((3,)),
            sem((3,)), sem((3,)),
        ],
        compiler_params=pltpu.CompilerParams(
            collective_id=0, has_side_effects=True, vmem_limit_bytes=48 * 2**20
        ),
        name="reshard",
    )(weights, placement)


KB = 32


def weave_kernel(place_ref, parts_ref, maxima_ref, out_ref, scales_ref, spread):
    @pl.when(pl.program_id(0) == 0)
    def _():
        row = lax.broadcasted_iota(jnp.int32, spread.shape, 0)
        col = lax.broadcasted_iota(jnp.int32, spread.shape, 1)
        hit = (row // 8 == col % KB) & (row % 8 == col // KB)
        spread[...] = jnp.where(hit, 1.0, 0.0).astype(jnp.bfloat16)
        for s in range(20):
            expert = place_ref[0, s]
            table = maxima_ref[:, expert // 4]
            which = expert % 4
            part = table[:, :, :32]
            for e in range(1, 4):
                part = jnp.where(which == e, table[:, :, 32 * e:32 * (e + 1)], part)
            for q in range(NX):
                scales_ref[0, s, ROW_TILES * q:ROW_TILES * (q + 1), :] = part[q, :ROW_TILES]

    for q in range(NX * ROW_TILES // 2):
        left = parts_ref[2 * q, 0].reshape(SLOTS_OWN * KB, TILE)
        right = parts_ref[2 * q + 1, 0].reshape(SLOTS_OWN * KB, TILE)
        both = jnp.concatenate([left, right], axis=1)
        woven = jnp.dot(spread[...], both, preferred_element_type=jnp.float32)
        woven = woven.reshape(KB, 8, 2 * TILE)[:, :SLOTS_OWN, :].astype(jnp.bfloat16)
        out_ref[0, :, :, pl.ds(q * 2 * TILE, 2 * TILE)] = woven


def weave(placement, parts, maxima):
    steps = 2 * TILE // KB
    per_tile = TILE // KB
    return pl.pallas_call(
        weave_kernel,
        out_shape=(
            jax.ShapeDtypeStruct((1, 2 * TILE, SLOTS_OWN, NX * ROW_TILES * TILE), jnp.bfloat16),
            jax.ShapeDtypeStruct((1, 20, NX * ROW_TILES, 32), jnp.float32),
        ),
        grid=(steps,),
        in_specs=[
            pl.BlockSpec(memory_space=pltpu.SMEM),
            pl.BlockSpec(
                (NX * ROW_TILES, 1, SLOTS_OWN, KB, TILE), lambda i: (0, i // per_tile, 0, i % per_tile, 0)
            ),
            pl.BlockSpec((NX, NY, 8, TILE), lambda i: (0, 0, 0, 0)),
        ],
        out_specs=(
            pl.BlockSpec((1, KB, SLOTS_OWN, NX * ROW_TILES * TILE), lambda i: (0, i, 0, 0)),
            pl.BlockSpec((1, 20, NX * ROW_TILES, 32), lambda i: (0, 0, 0, 0)),
        ),
        scratch_shapes=[pltpu.VMEM((8 * KB, SLOTS_OWN * KB), jnp.bfloat16)],
        compiler_params=pltpu.CompilerParams(vmem_limit_bytes=48 * 2**20),
        name="weave",
    )(placement, parts, maxima)


def on_device(weights, placement):
    parts, maxima = exchange(weights, placement)
    return weave(placement, parts, maxima)


def solution(mesh):
    in_specs = (P("group", "fsdp", None), P("group", None))
    out_specs = (P("group", "fsdp", None, None), P("group", None, None, None))
    return jax.shard_map(
        on_device, mesh=mesh, in_specs=in_specs, out_specs=out_specs, check_vma=False
    )
```

time: 574 us -> 143 us (0.25)
  the two profiles are of different devices: /device:TPU:128 before, /device:TPU:1 now
where the time goes in v1:
time: 143 us
  Pallas kernels  127 us (89%)
  local copies, waits for them, and re-layouts  15 us (10%)
    pallas_call x1, Pallas kernels, exchange(): pl.pallas_call(comm_kernel, out_shape=(jax.ShapeDtypeStruct((NX * ROW_TIL...  115 us
    pallas_call x1, local copies, waits for them, and re-layouts, weave(): pl.pallas_call(weave_kernel, out_shape=(jax.ShapeDtypeStruct((1, 2 * TILE...  12.9 us
    pallas_call x1, Pallas kernels, weave(): pl.pallas_call(weave_kernel, out_shape=(jax.ShapeDtypeStruct((1, 2 * TILE...  12.2 us

profile of v1, /device:TPU:1, one launch (start us, length us, event | category | flops | bytes accessed | tf_op | source)
XLA Modules:
  0.0 142.7 jit_solution(11009865238930603282)
XLA Ops:
  0.6 0.0 copy-start
  0.6 1.4 copy-done
  2.0 0.0 copy-start.1
  2.0 0.7 copy-done.1
  2.7 114.9 %reshard.1 = (bf16[24,2,5,128,128]{4,3,2,1,0:T(8,128)(2,1)}, f32[4,4,8,128]{3,2,1,0:T(8,128)S(1)}) custom-call(bf16[4,48,4096]{2,1,0:T(8,128)(2,1)S(1)} %copy-done, s32[1,20]{1,0:T(1,128)S(1)} %copy-done.1), custom_call_target="tpu_custom_call" | custom-call | tf_op jit(solution)/shard_map/reshard/pallas_call | solution.py:225
  117.6 12.2 %weave.1 = (bf16[1,256,5,3072]{3,2,1,0:T(8,128)(2,1)}, f32[1,20,24,32]{3,2,1,0:T(8,128)}) custom-call(s32[1,20]{1,0:T(1,128)S(1)} %copy-done.1, bf16[24,2,5,128,128]{4,3,2,1,0:T(8,128)(2,1)} %get-tuple-element.4.parts_ref, f32[4,4,8,128]{3,2,1,0:T(8,128)S(1)} %get-tuple-element.5.maxima_ref), custom_call_target="tpu_custom_call" | custom-call | tf_op jit(solution)/shard_map/weave/pallas_call | solution.py:287
  129.8 12.9 %copy.4 = bf16[1,256,5,3072]{3,1,2,0:T(8,128)(2,1)} copy(bf16[1,256,5,3072]{3,2,1,0:T(8,128)(2,1)} %get-tuple-element.6) | data formatting | bytes 15728640 | tf_op jit(solution)/shard_map/weave/pallas_call | solution.py:287
Async XLA Ops:
  0.6 1.4 copy-start
  2.0 0.7 copy-start.1

commit v2 on v1

v2 whole, which is shorter than its diff:
```python
import jax
import jax.numpy as jnp
from jax import lax
from jax.experimental import pallas as pl
from jax.experimental.pallas import tpu as pltpu
from jax.sharding import PartitionSpec as P

MESH = pl.DeviceIdType.MESH
TILE = 128
EPSILON = 1e-6
NX, NY, NZ = 4, 4, 8
NC = 16
EXPERTS_HERE = 4
SLOTS_OWN = 5
SLOTS = 20
ROWS_HERE = 48
ROW_TILES = 6
CHUNKS = 2 * ROW_TILES
SHARED = {10: 1, 11: -1}
GATHERS = CHUNKS + len(SHARED)
DIRECT = tuple(range(14))
SCHEDULE = (
    "c0", "o0", "n1", "h1", "z5", "z6", "c1", "s0", "o1", "h2", "c2", "z7", "z8", "s1", "o2", "c3",
    "o3", "h3", "z9", "z10", "s2", "z11", "z12", "c4", "o4", "s3", "z13", "z14", "c5", "o5", "s4",
    "c6", "o6", "c10", "c11", "s5", "c7", "o7", "s6", "c8", "o8", "r10", "s7", "c9", "o9", "r11",
    "s8", "o10", "o11", "mz", "s9", "s10", "my", "s11", "mx", "md",
)
Z_ORDER = [(0, 1)] + [(dz, dc) for dz in (7, 1, 6, 5, 4, 3, 2) for dc in (0, 1)]
X_ORDER = (2, 1, 3)
NEAR = 5
Y_ORDER = (2, 1, 3)


def block_of(out_ref, x, t, ct):
    rows = pl.ds(pl.multiple_of((x * ROW_TILES + t) * TILE, TILE), TILE)
    return out_ref.at[:, pl.ds(ct * TILE, TILE), rows]


def comm_kernel(w_hbm, place_ref, out_ref, maxima_ref, *scratch):
    ybufs = scratch[:GATHERS]
    (w_ref, w_sem, zbuf, staged, acc, zmax, ymax, xmax,
     z_send, z_recv, y_send, y_recv, x_send, x_recv, own_sem,
     sz_send, sz_recv, sy_send, sy_recv, sx_send, sx_recv, up_sem, down_sem) = scratch[GATHERS:]
    f = lax.axis_index("fsdp")
    y = lax.axis_index("group")
    x = f // NC
    c = f % NC
    z = c // 2
    core = c % 2

    def z_dev(step):
        dz, dc = step
        return 2 * ((z + dz) % NZ) + (core + dc) % 2

    def y_dev(dy):
        return (y + dy) % NY

    def x_dev(dx):
        return (x + dx) % NX

    fetch = pltpu.make_async_copy(w_hbm, w_ref, w_sem)
    fetch.start()
    barrier = pltpu.get_barrier_semaphore()
    for step in Z_ORDER[:NEAR]:
        pl.semaphore_signal(barrier, inc=1, device_id=(x * NC + z_dev(step), y), device_id_type=MESH)
    for d in Y_ORDER:
        pl.semaphore_signal(barrier, inc=1, device_id=(f, y_dev(d)), device_id_type=MESH)
    for d in X_ORDER:
        pl.semaphore_signal(barrier, inc=1, device_id=(x_dev(d) * NC + c, y), device_id_type=MESH)
    pl.semaphore_wait(barrier, NEAR + len(Y_ORDER) + len(X_ORDER))

    fetch.wait()
    waits = []

    def relay(level):
        if level:
            pl.semaphore_wait(up_sem.at[level - 1], 1)
            pl.semaphore_wait(down_sem.at[level - 1], 1)
        if level < 3:
            for dz, told in ((1, up_sem), (-1, down_sem)):
                pl.semaphore_signal(
                    told.at[level], inc=1, device_id=(x * NC + z_dev((dz, 0)), y), device_id_type=MESH
                )

    relay(0)
    def z_copy(k, ct):
        to = z_dev(Z_ORDER[k])
        cols = pl.ds(pl.multiple_of(to * (2 * TILE) + ct * TILE, TILE), TILE)
        rows = pl.ds(pl.multiple_of(c * ROWS_HERE, 16), ROWS_HERE)
        return pltpu.make_async_remote_copy(
            src_ref=w_ref.at[:, :, cols],
            dst_ref=zbuf.at[ct, :, rows, :],
            send_sem=z_send.at[ct, k],
            recv_sem=z_recv.at[ct, c],
            device_id=(x * NC + to, y),
            device_id_type=MESH,
        )

    def z_start(k, ct):
        copy = z_copy(k, ct)
        copy.start()
        waits.append(copy)

    for ct in range(2):
        cols = pl.ds(pl.multiple_of(c * (2 * TILE) + ct * TILE, TILE), TILE)
        rows = pl.ds(pl.multiple_of(c * ROWS_HERE, 16), ROWS_HERE)
        pltpu.make_async_copy(w_ref.at[:, :, cols], zbuf.at[ct, :, rows, :], z_recv.at[ct, c]).start()
    for k in range(5):
        z_start(k, 0)

    def z_wait(ct, first, last):
        def body(s, carry):
            rows = pl.ds(pl.multiple_of(s * ROWS_HERE, 16), ROWS_HERE)
            part = zbuf.at[ct, :, rows, :]
            pltpu.make_async_copy(part, part, z_recv.at[ct, s]).wait()
            return carry

        lax.fori_loop(first, last, body, 0)

    tile0 = (3 * z) // 4

    def tile_of(i):
        return (tile0 + i // 2) % ROW_TILES

    def first_source(t):
        return (8 * t) // 3

    def end_source(t):
        return (8 * t + 7) // 3 + 1

    acc[...] = jnp.zeros_like(acc)
    lane = lax.broadcasted_iota(jnp.int32, acc.shape, 1)
    sub = lax.broadcasted_iota(jnp.int32, acc.shape, 0)

    def shared_gather(i):
        return CHUNKS + sorted(SHARED).index(i)

    def experts_of(dy, first=0, count=EXPERTS_HERE):
        return pl.ds(y_dev(dy) * EXPERTS_HERE + first, count)

    def y_copy(g, n, to, experts):
        copy = pltpu.make_async_remote_copy(
            src_ref=ybufs[g].at[experts],
            dst_ref=ybufs[g].at[experts],
            send_sem=y_send.at[g, n],
            recv_sem=y_recv.at[g, n],
            device_id=(f, y_dev(to)),
            device_id_type=MESH,
        )
        copy.start()
        waits.append(copy)

    def y_wait(g, n, experts):
        part = ybufs[g].at[experts]
        pltpu.make_async_copy(part, part, y_recv.at[g, n]).wait()

    def y_spread(g):
        if g in DIRECT:
            y_copy(g, 2, 2, experts_of(0))
        y_copy(g, 0, 1, experts_of(0))
        y_copy(g, 1, -1, experts_of(0))

    def y_forward(g):
        if g in DIRECT:
            return
        y_wait(g, 0, experts_of(-1))
        y_copy(g, 2, 1, experts_of(-1, 0, 2))
        y_wait(g, 1, experts_of(1))
        y_copy(g, 3, -1, experts_of(1, 2, 2))

    def y_finish(g):
        if g in DIRECT:
            y_wait(g, 0, experts_of(-1))
            y_wait(g, 1, experts_of(1))
            y_wait(g, 2, experts_of(2))
        else:
            y_wait(g, 2, experts_of(2, 0, 2))
            y_wait(g, 3, experts_of(2, 2, 2))

    def share_copy(i):
        g = shared_gather(i)
        return pltpu.make_async_remote_copy(
            src_ref=ybufs[i].at[experts_of(0)],
            dst_ref=ybufs[g].at[experts_of(0)],
            send_sem=x_send.at[i, 2],
            recv_sem=x_recv.at[i, 2],
            device_id=(x_dev(SHARED[i]) * NC + c, y),
            device_id_type=MESH,
        )

    seen = set()

    def scale(i):
        order, ct = i // 2, i % 2
        t = tile_of(i)
        first, last = first_source(t), end_source(t)
        if ((order - 1) % ROW_TILES, ct) in seen:
            first = jnp.where(t > 0, jnp.maximum(first, end_source(t - 1)), first)
        if ((order + 1) % ROW_TILES, ct) in seen:
            last = jnp.where(t < ROW_TILES - 1, jnp.minimum(last, first_source(t + 1)), last)
        seen.add((order, ct))
        z_wait(ct, first, last)
        rows = pl.ds(pl.multiple_of(t * TILE, TILE), TILE)
        total = acc[...]
        for e in range(EXPERTS_HERE):
            block = zbuf[ct, e, rows, :].astype(jnp.float32)
            top = jnp.max(jnp.max(jnp.abs(block), axis=0, keepdims=True), axis=1, keepdims=True)
            code = (block / (top + EPSILON)).astype(jnp.bfloat16)
            ybufs[i][y * EXPERTS_HERE + e] = code.T
            at = (sub == t) & (lane == e * 32 + 2 * c + ct)
            total = jnp.where(at, top, total)
        acc[...] = total
        if i in SHARED:
            copy = share_copy(i)
            copy.start()
            waits.append(copy)

    def spread_shared(i):
        g = shared_gather(i)
        part = ybufs[g].at[experts_of(0)]
        pltpu.make_async_copy(part, part, x_recv.at[i, 2]).wait()
        y_spread(g)

    def select(i, n, g, owner):
        for j in range(SLOTS_OWN):
            expert = place_ref[0, owner * SLOTS_OWN + j]
            staged[i, n, j] = ybufs[g][expert]

    def x_copy(i, n, rows_of, owner):
        copy = pltpu.make_async_remote_copy(
            src_ref=staged.at[i, n],
            dst_ref=block_of(out_ref, rows_of, tile_of(i), i % 2),
            send_sem=x_send.at[i, n],
            recv_sem=x_recv.at[i, n],
            device_id=(owner * NC + c, y),
            device_id_type=MESH,
        )
        copy.start()
        waits.append(copy)

    def own_copy(i, n, k, rows_of):
        return pltpu.make_async_copy(
            staged.at[i, n], block_of(out_ref, rows_of, tile_of(i), i % 2), own_sem.at[i, k]
        )

    def select_and_send(i):
        y_finish(i)
        if i in SHARED:
            g, d = shared_gather(i), SHARED[i]
            select(i, 1, i, x_dev(-d))
            x_copy(i, 1, x, x_dev(-d))
            y_finish(g)
            select(i, 0, g, x_dev(d))
            x_copy(i, 0, x_dev(-d), x_dev(d))
            select(i, 2, i, x)
            own_copy(i, 2, 0, x).start()
            select(i, 3, g, x)
            own_copy(i, 3, 1, x_dev(-d)).start()
        else:
            for n, d in enumerate(X_ORDER):
                select(i, n, i, x_dev(d))
                x_copy(i, n, x, x_dev(d))
            select(i, 3, i, x)
            own_copy(i, 3, 0, x).start()

    def maxima_copy(ref, here, to, send, recv):
        return pltpu.make_async_remote_copy(
            src_ref=ref.at[here], dst_ref=ref.at[here], send_sem=send, recv_sem=recv,
            device_id=to, device_id_type=MESH,
        )

    def maxima_wait(ref, source, recv):
        part = ref.at[source]
        pltpu.make_async_copy(part, part, recv).wait()

    def maxima_z_send():
        zmax[c] = acc[...]
        for k, step in enumerate(Z_ORDER):
            copy = maxima_copy(zmax, c, (x * NC + z_dev(step), y), sz_send.at[k], sz_recv.at[c])
            copy.start()
            waits.append(copy)

    def maxima_y_send():
        for k, step in enumerate(Z_ORDER):
            maxima_wait(zmax, z_dev(step), sz_recv.at[z_dev(step)])
        ymax[y] = jnp.max(zmax[...], axis=0)
        for n, d in enumerate(Y_ORDER):
            copy = maxima_copy(ymax, y, (f, y_dev(d)), sy_send.at[n], sy_recv.at[n])
            copy.start()
            waits.append(copy)

    def maxima_x_send():
        for n, d in enumerate(Y_ORDER):
            maxima_wait(ymax, (y - d) % NY, sy_recv.at[n])
        xmax[x] = ymax[...]
        for n, d in enumerate(X_ORDER):
            copy = maxima_copy(xmax, x, (x_dev(d) * NC + c, y), sx_send.at[n], sx_recv.at[n])
            copy.start()
            waits.append(copy)

    def maxima_done():
        for n, d in enumerate(X_ORDER):
            maxima_wait(xmax, (x - d) % NX, sx_recv.at[n])
        maxima_ref[...] = xmax[...]

    for step in SCHEDULE:
        if step == "mz":
            maxima_z_send()
        elif step == "my":
            maxima_y_send()
        elif step == "mx":
            maxima_x_send()
        elif step == "md":
            maxima_done()
        else:
            act, i = step[0], int(step[1:])
            if act == "h":
                relay(i)
            elif act == "n":
                for k in range(5):
                    z_start(k, 1)
            elif act == "z":
                for ct in range(2):
                    z_start(i, ct)
            elif act == "c":
                scale(i)
            elif act == "o":
                y_spread(i)
            elif act == "r":
                spread_shared(i)
            elif act == "f":
                y_forward(i)
            elif act == "g":
                y_forward(shared_gather(i))
            else:
                select_and_send(i)

    for copy in waits:
        copy.wait_send()
    def x_wait(i, n, rows_of):
        part = block_of(out_ref, rows_of, tile_of(i), i % 2)
        pltpu.make_async_copy(part, part, x_recv.at[i, n]).wait()

    for i in range(CHUNKS):
        if i in SHARED:
            d = SHARED[i]
            x_wait(i, 1, x_dev(d))
            x_wait(i, 0, x_dev(2))
            own_copy(i, 2, 0, x).wait()
            own_copy(i, 3, 1, x_dev(-d)).wait()
        else:
            for n, d in enumerate(X_ORDER):
                x_wait(i, n, x_dev(-d))
            own_copy(i, 3, 0, x).wait()


def exchange(weights, placement):
    sem = pltpu.SemaphoreType.DMA
    return pl.pallas_call(
        comm_kernel,
        out_shape=(
            pltpu.VMEM((SLOTS_OWN, 2 * TILE, NX * ROW_TILES * TILE), jnp.bfloat16),
            pltpu.VMEM((NX, NY, 8, TILE), jnp.float32),
        ),
        in_specs=[pl.BlockSpec(memory_space=pltpu.HBM), pl.BlockSpec(memory_space=pltpu.SMEM)],
        out_specs=(pl.BlockSpec(memory_space=pltpu.VMEM), pl.BlockSpec(memory_space=pltpu.VMEM)),
        scratch_shapes=[pltpu.VMEM((16, TILE, TILE), jnp.bfloat16)] * GATHERS
        + [
            pltpu.VMEM((EXPERTS_HERE, ROWS_HERE, 2 * TILE * NC), jnp.bfloat16),
            sem,
            pltpu.VMEM((2, EXPERTS_HERE, ROW_TILES * TILE, TILE), jnp.bfloat16),
            pltpu.VMEM((CHUNKS, 4, SLOTS_OWN, TILE, TILE), jnp.bfloat16),
            pltpu.VMEM((8, TILE), jnp.float32),
            pltpu.VMEM((NC, 8, TILE), jnp.float32),
            pltpu.VMEM((NY, 8, TILE), jnp.float32),
            pltpu.VMEM((NX, NY, 8, TILE), jnp.float32),
            sem((2, 15)), sem((2, NC)),
            sem((GATHERS, 4)), sem((GATHERS, 4)),
            sem((CHUNKS, 3)), sem((CHUNKS, 3)), sem((CHUNKS, 2)),
            sem((15,)), sem((NC,)),
            sem((3,)), sem((3,)),
            sem((3,)), sem((3,)),
            pltpu.SemaphoreType.REGULAR((3,)), pltpu.SemaphoreType.REGULAR((3,)),
        ],
        compiler_params=pltpu.CompilerParams(
            collective_id=0, has_side_effects=True, vmem_limit_bytes=40 * 2**20
        ),
        name="reshard",
    )(weights, placement)


PIECES = 8


def finish_kernel(place_ref, codes_ref, maxima_ref, out_ref, scales_ref, sems):
    rows = 2 * TILE // PIECES
    copies = []
    for q in range(PIECES):
        part = pl.ds(q * rows, rows)
        copy = pltpu.make_async_copy(codes_ref.at[:, part], out_ref.at[:, part], sems.at[q])
        copy.start()
        copies.append(copy)
    for s in range(SLOTS):
        expert = place_ref[0, s]
        which = expert % EXPERTS_HERE
        table = maxima_ref[:, expert // EXPERTS_HERE]
        part = table[:, :, :32]
        for e in range(1, EXPERTS_HERE):
            part = jnp.where(which == e, table[:, :, 32 * e:32 * (e + 1)], part)
        for q in range(NX):
            scales_ref[0, s, ROW_TILES * q:ROW_TILES * (q + 1), :] = part[q, :ROW_TILES]
    for copy in copies:
        copy.wait()


def finish(placement, codes, maxima):
    return pl.pallas_call(
        finish_kernel,
        out_shape=(
            jax.ShapeDtypeStruct(codes.shape, codes.dtype),
            jax.ShapeDtypeStruct((1, SLOTS, NX * ROW_TILES, 32), jnp.float32),
        ),
        in_specs=[
            pl.BlockSpec(memory_space=pltpu.SMEM),
            pl.BlockSpec(memory_space=pl.ANY),
            pl.BlockSpec(memory_space=pltpu.VMEM),
        ],
        out_specs=(pl.BlockSpec(memory_space=pl.ANY), pl.BlockSpec(memory_space=pltpu.VMEM)),
        scratch_shapes=[pltpu.SemaphoreType.DMA((PIECES,))],
        compiler_params=pltpu.CompilerParams(vmem_limit_bytes=16 * 2**20),
        name="finish",
    )(placement, codes, maxima)


def on_device(weights, placement):
    weights = pltpu.with_memory_space_constraint(weights, pltpu.HBM)
    placement = pltpu.with_memory_space_constraint(placement, pltpu.HBM)
    codes, maxima = exchange(weights, placement)
    codes, scales = finish(placement, codes, maxima)
    return jnp.transpose(codes, (1, 0, 2))[None], scales


def solution(mesh):
    in_specs = (P("group", "fsdp", None), P("group", None))
    out_specs = (P("group", "fsdp", None, None), P("group", None, None, None))
    return jax.shard_map(
        on_device, mesh=mesh, in_specs=in_specs, out_specs=out_specs, check_vma=False
    )
```

time: 143 us -> 119 us (0.83)
  the two profiles are of different devices: /device:TPU:1 before, /device:TPU:32 now
where the time goes in v2:
time: 119 us
  Pallas kernels  118 us (99%)
    pallas_call x1, Pallas kernels, exchange(): pl.pallas_call(comm_kernel, out_shape=(pltpu.VMEM((SLOTS_OWN, 2 * TILE, N...  113 us
    pallas_call x1, Pallas kernels, finish(): pl.pallas_call(finish_kernel, out_shape=(jax.ShapeDtypeStruct(codes.shape...  5.02 us

profile of v2, /device:TPU:32, one launch (start us, length us, event | category | flops | bytes accessed | tf_op | source)
XLA Modules:
  0.0 118.7 jit_solution(5550345143146694319)
XLA Ops:
  0.6 113.0 %reshard.1 = (bf16[5,256,3072]{2,1,0:T(8,128)(2,1)S(1)}, f32[4,4,8,128]{3,2,1,0:T(8,128)S(1)}) custom-call(bf16[4,48,4096]{2,1,0:T(8,128)(2,1)} %w_hbm.1, s32[1,20]{1,0:T(1,128)} %place_ref.3), custom_call_target="tpu_custom_call" | custom-call | tf_op jit(solution)/shard_map/reshard/pallas_call | solution.py:359
  113.7 5.0 %finish.1 = (bf16[5,256,3072]{2,1,0:T(8,128)(2,1)}, f32[1,20,24,32]{3,2,1,0:T(8,128)}) custom-call(s32[1,20]{1,0:T(1,128)} %place_ref.3, bf16[5,256,3072]{2,1,0:T(8,128)(2,1)S(1)} %get-tuple-element.6.codes_ref, f32[4,4,8,128]{3,2,1,0:T(8,128)S(1)} %get-tuple-element.7.maxima_ref), custom_call_target="tpu_custom_call" | custom-call | tf_op jit(solution)/shard_map/finish/pallas_call | solution.py:417

commit v3 on v2

--- a/solution.py
+++ b/solution.py
@@ -20,10 +20,10 @@
 GATHERS = CHUNKS + len(SHARED)
 DIRECT = tuple(range(14))
 SCHEDULE = (
-    "c0", "o0", "n1", "h1", "z5", "z6", "c1", "s0", "o1", "h2", "c2", "z7", "z8", "s1", "o2", "c3",
-    "o3", "h3", "z9", "z10", "s2", "z11", "z12", "c4", "o4", "s3", "z13", "z14", "c5", "o5", "s4",
+    "c0", "o0", "n1", "h1", "z5", "z6", "h2", "z7", "z8", "c1", "o1", "h3", "z9", "z10", "s0", "c2",
+    "o2", "z11", "z12", "s1", "z13", "z14", "c3", "o3", "s2", "c4", "o4", "s3", "c5", "o5", "s4",
     "c6", "o6", "c10", "c11", "s5", "c7", "o7", "s6", "c8", "o8", "r10", "s7", "c9", "o9", "r11",
-    "s8", "o10", "o11", "mz", "s9", "s10", "my", "s11", "mx", "md",
+    "mz", "s8", "o10", "o11", "my", "s9", "s10", "mx", "s11", "md",
 )
 Z_ORDER = [(0, 1)] + [(dz, dc) for dz in (7, 1, 6, 5, 4, 3, 2) for dc in (0, 1)]
 X_ORDER = (2, 1, 3)

time: 119 us -> 117 us (0.983)
  the two profiles are of different devices: /device:TPU:32 before, /device:TPU:128 now
where the time goes in v3:
time: 117 us
  Pallas kernels  116 us (99%)
    pallas_call x1, Pallas kernels, exchange(): pl.pallas_call(comm_kernel, out_shape=(pltpu.VMEM((SLOTS_OWN, 2 * TILE, N...  111 us
    pallas_call x1, Pallas kernels, finish(): pl.pallas_call(finish_kernel, out_shape=(jax.ShapeDtypeStruct(codes.shape...  5.02 us

profile of v3, /device:TPU:128, one launch (start us, length us, event | category | flops | bytes accessed | tf_op | source)
XLA Modules:
  0.0 116.7 jit_solution(3219807149361279315)
XLA Ops:
  0.6 111.0 %reshard.1 = (bf16[5,256,3072]{2,1,0:T(8,128)(2,1)S(1)}, f32[4,4,8,128]{3,2,1,0:T(8,128)S(1)}) custom-call(bf16[4,48,4096]{2,1,0:T(8,128)(2,1)} %w_hbm.1, s32[1,20]{1,0:T(1,128)} %place_ref.3), custom_call_target="tpu_custom_call" | custom-call | tf_op jit(solution)/shard_map/reshard/pallas_call | solution.py:359
  111.6 5.0 %finish.1 = (bf16[5,256,3072]{2,1,0:T(8,128)(2,1)}, f32[1,20,24,32]{3,2,1,0:T(8,128)}) custom-call(s32[1,20]{1,0:T(1,128)} %place_ref.3, bf16[5,256,3072]{2,1,0:T(8,128)(2,1)S(1)} %get-tuple-element.6.codes_ref, f32[4,4,8,128]{3,2,1,0:T(8,128)S(1)} %get-tuple-element.7.maxima_ref), custom_call_target="tpu_custom_call" | custom-call | tf_op jit(solution)/shard_map/finish/pallas_call | solution.py:417

commit v4 on v3

--- a/solution.py
+++ b/solution.py
@@ -20,10 +20,10 @@
 GATHERS = CHUNKS + len(SHARED)
 DIRECT = tuple(range(14))
 SCHEDULE = (
-    "c0", "o0", "n1", "h1", "z5", "z6", "h2", "z7", "z8", "c1", "o1", "h3", "z9", "z10", "s0", "c2",
-    "o2", "z11", "z12", "s1", "z13", "z14", "c3", "o3", "s2", "c4", "o4", "s3", "c5", "o5", "s4",
-    "c6", "o6", "c10", "c11", "s5", "c7", "o7", "s6", "c8", "o8", "r10", "s7", "c9", "o9", "r11",
-    "mz", "s8", "o10", "o11", "my", "s9", "s10", "mx", "s11", "md",
+    "c0", "o0", "n1", "h1", "z5", "z6", "h2", "z7", "z8", "c1", "o1", "h3", "z9", "z10", "z11",
+    "z12", "z13", "z14", "s0", "c2", "o2", "s1", "c3", "o3", "s2", "c4", "o4", "s3", "c5", "o5",
+    "s4", "c10", "c11", "c6", "o6", "s5", "c7", "o7", "s6", "c8", "o8", "r10", "s7", "c9", "o9",
+    "r11", "mz", "s8", "o10", "o11", "my", "s9", "s10", "mx", "s11", "md",
 )
 Z_ORDER = [(0, 1)] + [(dz, dc) for dz in (7, 1, 6, 5, 4, 3, 2) for dc in (0, 1)]
 X_ORDER = (2, 1, 3)

time: 117 us -> 117 us (level)
  no operation moved by 1% of the time
where the time goes in v4:
time: 117 us
  Pallas kernels  116 us (99%)
    pallas_call x1, Pallas kernels, exchange(): pl.pallas_call(comm_kernel, out_shape=(pltpu.VMEM((SLOTS_OWN, 2 * TILE, N...  111 us
    pallas_call x1, Pallas kernels, finish(): pl.pallas_call(finish_kernel, out_shape=(jax.ShapeDtypeStruct(codes.shape...  5.02 us

profile of v4, /device:TPU:128, one launch (start us, length us, event | category | flops | bytes accessed | tf_op | source)
XLA Modules:
  0.0 116.7 jit_solution(15234369572406301562)
XLA Ops:
  0.6 111.0 %reshard.1 = (bf16[5,256,3072]{2,1,0:T(8,128)(2,1)S(1)}, f32[4,4,8,128]{3,2,1,0:T(8,128)S(1)}) custom-call(bf16[4,48,4096]{2,1,0:T(8,128)(2,1)} %w_hbm.1, s32[1,20]{1,0:T(1,128)} %place_ref.3), custom_call_target="tpu_custom_call" | custom-call | tf_op jit(solution)/shard_map/reshard/pallas_call | solution.py:359
  111.6 5.0 %finish.1 = (bf16[5,256,3072]{2,1,0:T(8,128)(2,1)}, f32[1,20,24,32]{3,2,1,0:T(8,128)}) custom-call(s32[1,20]{1,0:T(1,128)} %place_ref.3, bf16[5,256,3072]{2,1,0:T(8,128)(2,1)S(1)} %get-tuple-element.6.codes_ref, f32[4,4,8,128]{3,2,1,0:T(8,128)S(1)} %get-tuple-element.7.maxima_ref), custom_call_target="tpu_custom_call" | custom-call | tf_op jit(solution)/shard_map/finish/pallas_call | solution.py:417
